TPU v7x, 256 devices: a whole 4x4x8 slice. The times are simulated.
256 devices in a mesh: rep: 32 (over y, x, core), pre: 8 (over z).
Axes of the slice: x: 4, y: 4, z: 8, core: 2. Of those that a mesh axis runs over, the one named last changes fastest.
Arguments:
- queries: bfloat16 [4, 1024, 64, 128], P(None, 'rep', 'pre'), may hold values from -20 to 20
- newest_key_value: bfloat16 [4, 1024, 8, 256], P(None, 'rep', 'pre'), may hold values from -15 to 15
- prefix_kv: bfloat16 [8, 16384, 256], P(None, 'pre'), may hold values from -96 to 96
- suffix_pool: bfloat16 [1792, 8, 128, 256], P('rep', 'pre'), may hold values from -96 to 96
- page_table: int32 [1024, 2], P('rep'), may hold values from 0 to 55, as said below
- suffix_pages: int32 [1024], P('rep'), may hold values from 1 to 2, as said below
- arrival: int32 [1024], P('rep'), may hold values from 0 to 1023, as said below
Outputs:
- attended: bfloat16 [4, 1024, 64, 128], P(None, 'rep', 'pre')
Inputs may be any that keep to these rules, and one draw needn't show every extreme that they name: Position j of the new layout holds the agent that stood at position arrival[j] of the old one; every position appears once; each replica sends exactly 16 of its agents to other replicas, at most one to any single replica. An agent's suffix holds suffix_pages whole pages of 128 tokens; the values of the 32 agents of one replica sum to 56. `page_table`: row a lists, in order, the pages of agent a in its own replica's pool; entries k >= suffix_pages[a] are unused; used entries of one replica never coincide.
All inputs are finite; a program needn't handle non-finite values.
Results may differ from a plain program's by a relative error of at most 0.0027.
Values may be sent and summed in bfloat16 or wider, within the bound.
A program may use at most 128 MiB of HBM per device.

v0:
```python
import jax
import jax.numpy as jnp
from jax import lax
from jax.sharding import PartitionSpec as P

negative_fill = -1e30


def prefix_partial(gathered, prefix_kv, score_scale):
    step_count, agents, head_count, head_dim = gathered.shape
    kv_heads = prefix_kv.shape[0]
    grouping_size = head_count // kv_heads
    query_rows = gathered.reshape(step_count, agents, kv_heads, grouping_size, head_dim).transpose(
        2, 0, 1, 3, 4
    )
    query_rows = query_rows.reshape(kv_heads, step_count * agents * grouping_size, head_dim)

    def per_head(pair_item):
        block_of_queries, head_kv = pair_item
        scores = (
            lax.dot_general(
                block_of_queries,
                head_kv[:, :head_dim],
                (((1,), (1,)), ((), ())),
                preferred_element_type=jnp.float32,
            )
            * score_scale
        )
        peak_score = jnp.max(scores, axis=1)
        weights = jnp.exp(scores - peak_score[:, None])
        weight_sum = jnp.sum(weights, axis=1)
        partial_value = (
            jnp.dot(
                weights.astype(jnp.bfloat16),
                head_kv[:, head_dim:],
                preferred_element_type=jnp.float32,
            )
            / weight_sum[:, None]
        )
        return (partial_value, peak_score + jnp.log(weight_sum))

    partial_value, log_total = lax.map(per_head, (query_rows, prefix_kv))
    partial_value = partial_value.reshape(
        kv_heads, step_count, agents, grouping_size, head_dim
    ).transpose(1, 2, 0, 3, 4)
    log_total = log_total.reshape(kv_heads, step_count, agents, grouping_size).transpose(1, 2, 0, 3)
    return (
        partial_value.reshape(step_count, agents, head_count, head_dim),
        log_total.reshape(step_count, agents, head_count),
    )


def suffix_partial(queries, cache_of_suffix, newest_key_value, lengths, score_scale):
    step_count, agents, head_count, head_dim = queries.shape
    page_count = cache_of_suffix.shape[1]
    kv_heads = cache_of_suffix.shape[2]
    page_size = cache_of_suffix.shape[3]
    grouping_size = head_count // kv_heads
    tokens_in_cache = page_count * page_size
    cached_entries = cache_of_suffix.transpose(0, 2, 1, 3, 4).reshape(
        agents, kv_heads, tokens_in_cache, 2 * head_dim
    )
    recent = newest_key_value.transpose(1, 2, 0, 3)
    key_values = jnp.concatenate([cached_entries, recent], axis=2)
    grouped = queries.reshape(step_count, agents, kv_heads, grouping_size, head_dim)
    scores = (
        jnp.einsum(
            "sahgd,ahkd->sahgk",
            grouped,
            key_values[..., :head_dim],
            preferred_element_type=jnp.float32,
        )
        * score_scale
    )
    token_ids = jnp.arange(tokens_in_cache + step_count, dtype=jnp.int32)
    step_ids = jnp.arange(step_count, dtype=jnp.int32)
    in_cache = token_ids[None, :] < (lengths * page_size)[:, None]
    in_fresh = (token_ids[None, :] >= tokens_in_cache) & (
        token_ids[None, :] - tokens_in_cache <= step_ids[:, None]
    )
    usable = (in_cache[None, :, :] | in_fresh[:, None, :])[:, :, None, None, :]
    scores = jnp.where(usable, scores, negative_fill)
    peak_score = jnp.max(scores, axis=-1)
    weights = jnp.where(usable, jnp.exp(scores - peak_score[..., None]), 0.0)
    weight_sum = jnp.sum(weights, axis=-1)
    partial_value = (
        jnp.einsum(
            "sahgk,ahkd->sahgd",
            weights.astype(jnp.bfloat16),
            key_values[..., head_dim:],
            preferred_element_type=jnp.float32,
        )
        / weight_sum[..., None]
    )
    log_total = peak_score + jnp.log(weight_sum)
    return (
        partial_value.reshape(step_count, agents, head_count, head_dim),
        log_total.reshape(step_count, agents, head_count),
    )


def per_device(
    queries, newest_key_value, prefix_kv, suffix_pool, page_table, suffix_pages, arrival
):
    step_count, agents, head_dev, head_dim = queries.shape
    score_scale = head_dim ** (-0.5)
    rep_count = lax.axis_size("rep")
    pre_count = lax.axis_size("pre")
    my_rep = lax.axis_index("rep")
    page_count = page_table.shape[1]
    pool_pages = suffix_pool.shape[0]
    everyone, all_lengths = (
        lax.all_gather(arrival, "rep", axis=0, tiled=True),
        lax.all_gather(suffix_pages, "rep", axis=0, tiled=True),
    )
    my_agents = lax.dynamic_slice_in_dim(everyone, my_rep * agents, agents)
    source_rep = my_agents // agents
    old_slot = my_agents % agents
    staying = source_rep == my_rep
    new_lengths = all_lengths[my_agents]
    new_layout = everyone.reshape(rep_count, agents)
    peer_ids = jnp.arange(rep_count, dtype=jnp.int32)
    leaving = (new_layout // agents == my_rep) & (peer_ids[:, None] != my_rep)
    has_leaver = jnp.any(leaving, axis=1)
    leaver_slot = jnp.sum(jnp.where(leaving, new_layout % agents, 0), axis=1)
    leaver_length = suffix_pages[leaver_slot]
    page_ids = jnp.arange(page_count, dtype=jnp.int32)
    gathered = lax.all_gather(queries, "pre", axis=2, tiled=True)
    prefix_out, prefix_lse = prefix_partial(gathered, prefix_kv, score_scale)
    live_pages = has_leaver[:, None] & (page_ids[None, :] < leaver_length[:, None])
    outgoing = suffix_pool[page_table[leaver_slot]]
    outgoing = jnp.where(live_pages[:, :, None, None, None], outgoing, jnp.zeros((), jnp.bfloat16))
    arrived = lax.all_to_all(outgoing, "rep", split_axis=0, concat_axis=0, tiled=True)
    combined = jnp.concatenate(
        [suffix_pool, arrived.reshape((rep_count * page_count,) + suffix_pool.shape[1:])], axis=0
    )
    page_index = jnp.where(
        staying[:, None],
        page_table[old_slot],
        pool_pages + source_rep[:, None] * page_count + page_ids[None, :],
    )
    cache_of_suffix = combined[page_index]
    suffix_out, suffix_lse = suffix_partial(
        queries, cache_of_suffix, newest_key_value, new_lengths, score_scale
    )
    shares_out = prefix_out.reshape(step_count, agents, pre_count, head_dev, head_dim)
    shares_lse = prefix_lse.reshape(step_count, agents, pre_count, head_dev)
    got_out, got_lse = (
        lax.all_to_all(shares_out, "pre", split_axis=2, concat_axis=2, tiled=True),
        lax.all_to_all(shares_lse, "pre", split_axis=2, concat_axis=2, tiled=True),
    )
    every_lse = jnp.concatenate([got_lse, suffix_lse[:, :, None, :]], axis=2)
    peak_lse = jnp.max(every_lse, axis=2)
    total_lse = peak_lse + jnp.log(jnp.sum(jnp.exp(every_lse - peak_lse[:, :, None, :]), axis=2))
    shard_weights = jnp.exp(got_lse - total_lse[:, :, None, :])
    result = jnp.sum(shard_weights[..., None] * got_out, axis=2)
    result = result + jnp.exp(suffix_lse - total_lse)[..., None] * suffix_out
    return result.astype(jnp.bfloat16)


def solution(mesh):
    return jax.shard_map(
        per_device,
        mesh=mesh,
        in_specs=(
            P(None, "rep", "pre", None),
            P(None, "rep", "pre", None),
            P(None, "pre", None),
            P("rep", "pre", None, None),
            P("rep", None),
            P("rep"),
            P("rep"),
        ),
        out_specs=P(None, "rep", "pre", None),
        check_vma=False,
    )
```

profile of v0, /device:TPU:1, one launch (start us, length us, event | category | flops | bytes accessed | tf_op | source)
XLA Modules:
  0.0 300.5 jit_solution(7561437633924815574)
XLA Ops:
  6.5 0.7 all-gather.2.cloned.1.call-update
  7.3 0.8 copy.75
  8.0 1.3 dynamic-slice
  10.0 0.9 dynamic-update-slice.1
  10.8 0.8 dynamic-update-slice
  11.7 14.7 %all-reduce.2 = (s32[1024]{0:T(1024)S(1)}, s32[1024]{0:T(1024)S(1)}) all-reduce(s32[1024]{0:T(1024)S(1)} %dynamic-update-slice.1, s32[1024]{0:T(1024)S(1)} %dynamic-update-slice), channel_id=1, replica_groups=mesh['rep'=32,'pre'=8] {'rep'}, use_global_device_ids=true, to_apply=%add.1 | all-reduce | flops 2048 | bytes 16384
  26.8 1.4 gather_fusion.1
  28.1 0.6 gather_fusion.2
  29.0 4.8 %gather_fusion.3 = bf16[64,128,256]{2,1,0:T(8,128)(2,1)} fusion(bf16[56,128,256]{2,1,0:T(8,128)(2,1)} %bitcast.121, s32[1024]{0:T(1024)S(1)} %pad_clamp_fusion.2), kind=kCustom, calls=%fused_computation.3 | custom fusion | bytes 8388864 | tf_op jit(solution)/shard_map/gather | solution.py:131
  33.9 22.5 %all-gather.2.cloned.1.call-done = bf16[4,32,64,128]{3,2,1,0:T(8,128)(2,1)} async-done(((bf16[4,32,8,128]{3,2,1,0:T(8,128)(2,1)}), bf16[4,32,64,128]{3,2,1,0:T(8,128)(2,1)}) %all-gather.2.cloned.1.call-update) | async-done | bytes 2097168 | tf_op jit(solution)/shard_map/all_gather | solution.py:128
  56.3 2.2 copy.73
  58.5 55.8 %while.12 = (s32[]{:T(128)}, f32[8,1024,128]{2,1,0:T(8,128)}, f32[8,1024]{1,0:T(8,128)S(1)}, bf16[8,1024,128]{2,1,0:T(8,128)(2,1)S(1)}, bf16[8,2048,256]{2,1,0:T(8,128)(2,1)}, /*index=5*/s32[]{:T(128)}, s32[]{:T(128)}) while((s32[]{:T(128)}, f32[8,1024,128]{2,1,0:T(8,128)}, f32[8,1024]{1,0:T(8,128)S(1)}, bf16[8,1024,128]{2,1,0:T(8,128)(2,1)S(1)}, ...), condition=%wide.region_3.4_spmd, body=%wide.region_0.3_spmd.sunk | while | flops 1090649088 | bytes 29139044 | solution.py:42
  58.5 1.3 dynamic-slice_bitcast_fusion.2
  59.8 1.3 multiply_reduce_fusion.3
  61.2 1.9 fusion.83
  63.1 2.3 fusion.84
  65.5 1.3 dynamic-slice_bitcast_fusion.2
  66.8 1.3 multiply_reduce_fusion.3
  68.1 1.9 fusion.83
  70.1 2.3 fusion.84
  72.5 1.3 dynamic-slice_bitcast_fusion.2
  73.8 1.3 multiply_reduce_fusion.3
  75.1 1.9 fusion.83
  77.1 2.3 fusion.84
  79.5 1.3 dynamic-slice_bitcast_fusion.2
  80.8 1.3 multiply_reduce_fusion.3
  82.1 1.9 fusion.83
  84.1 2.3 fusion.84
  86.4 1.3 dynamic-slice_bitcast_fusion.2
  87.7 1.3 multiply_reduce_fusion.3
  89.1 1.9 fusion.83
  91.0 2.3 fusion.84
  93.4 1.3 dynamic-slice_bitcast_fusion.2
  94.7 1.3 multiply_reduce_fusion.3
  96.0 1.9 fusion.83
  98.0 2.3 fusion.84
  100.4 1.3 dynamic-slice_bitcast_fusion.2
  101.7 1.3 multiply_reduce_fusion.3
  103.0 1.9 fusion.83
  105.0 2.3 fusion.84
  107.4 1.3 dynamic-slice_bitcast_fusion.2
  108.7 1.3 multiply_reduce_fusion.3
  110.0 1.9 fusion.83
  111.9 2.3 fusion.84
  114.3 0.3 reshape.339
  114.8 0.7 reshape.418
  115.6 3.7 %all-to-all-start = ((f32[8,1,1024]{2,1,0:T(1,128)}), f32[8,1,1024]{2,1,0:T(1,128)S(1)}, u32[]{:S(2)}, u32[]{:S(2)}) async-start(f32[8,1,1024]{2,1,0:T(1,128)} %reshape.418), calls=%async_computation | async-start | bytes 65536 | tf_op jit(solution)/shard_map/all_to_all | solution.py:150
  119.3 4.5 %broadcast_select_fusion = bf16[32,2,1,128,256]{4,3,1,2,0:T(8,128)(2,1)} fusion(bf16[32,2,1,128,256]{4,3,1,2,0:T(8,128)(2,1)} %bitcast.123, pred[32,2]{1,0:T(8,128)(4,1)S(1)} %fusion.62), kind=kLoop, calls=%fused_computation.27 | loop fusion | flops 2097152 | bytes 8388672 | tf_op jit(solution)/shard_map/jit(_where)/select_n | solution.py:132
  123.8 2.4 all-to-all-done
  126.1 65.4 %all_to_all.15 = bf16[32,2,1,128,256]{4,3,1,2,0:T(8,128)(2,1)} all-to-all(bf16[32,2,1,128,256]{4,3,1,2,0:T(8,128)(2,1)} %broadcast_select_fusion), channel_id=1, replica_groups=mesh['rep'=32,'pre'=8] {'rep'}, dimensions={0} | all-to-all | bytes 8388608 | tf_op jit(solution)/shard_map/all_to_all | solution.py:133
  191.5 4.7 %all-to-all-start.2 = ((f32[4,32,8,8,128]{4,3,1,0,2:T(8,128)}), f32[4,32,8,8,128]{4,3,1,0,2:T(8,128)}, u32[]{:S(2)}, u32[]{:S(2)}) async-start(f32[4,32,8,8,128]{4,3,1,0,2:T(8,128)} %bitcast.126), calls=%async_computation.2 | async-start | bytes 8388608 | tf_op jit(solution)/shard_map/all_to_all | solution.py:149
  196.4 0.6 gather_fusion.4
  197.3 0.7 gather_fusion
  198.2 0.5 broadcast.303
  198.7 0.7 reduce.4
  199.5 7.1 %maximum_bitcast_fusion = bf16[120,128,256]{2,1,0:T(8,128)(2,1)} fusion(bf16[64,1,128,256]{3,2,0,1:T(8,128)(2,1)} %bitcast.124, bf16[56,1,128,256]{3,2,0,1:T(8,128)(2,1)} %bitcast.122), kind=kLoop, calls=%fused_computation.23 | loop fusion | flops 3932160 | bytes 15728640 | tf_op jit(solution)/shard_map/concatenate | solution.py:134
  206.6 6.0 %gather_fusion.5 = bf16[64,128,256]{2,1,0:T(8,128)(2,1)} fusion(bf16[120,128,256]{2,1,0:T(8,128)(2,1)} %maximum_bitcast_fusion, s32[1024]{0:T(1024)S(1)} %pad_clamp_fusion), kind=kCustom, calls=%fused_computation.5 | custom fusion | bytes 8388864 | tf_op jit(solution)/shard_map/gather | solution.py:142
  212.6 2.6 fusion.74
  215.3 0.7 fusion.31
  216.5 72.0 %all-to-all-done.2 = f32[4,32,8,8,128]{4,3,1,0,2:T(8,128)} async-done(((f32[4,32,8,8,128]{4,3,1,0,2:T(8,128)}), f32[4,32,8,8,128]{4,3,1,0,2:T(8,128)}, u32[]{:S(2)}, u32[]{:S(2)}) %all-to-all-start.2) | async-done | bytes 4194336 | tf_op jit(solution)/shard_map/all_to_all | solution.py:149
  288.6 3.0 %multiply_reduce_fusion.1 = f32[4,32,8,128]{3,2,1,0:T(8,128)S(1)} fusion(f32[4,32,8,8,128]{4,3,1,0,2:T(8,128)} %all-to-all-done.2, f32[4,32,8,8]{3,1,0,2:T(8,128)S(1)} %copy.88), kind=kLoop, calls=%fused_computation.26 | loop fusion | flops 1966080 | bytes 4751360 | tf_op jit(solution)/shard_map/reduce_sum | solution.py:156
  291.6 0.4 copy-done
  292.0 0.9 fusion.47
  292.9 0.7 copy.91
  (66 shorter events, 2.9 us)
Async XLA Ops:
  6.5 49.8 %all-gather.2.cloned.1.call-start = ((), (), s32[]{:S(2)}) async-start(), calls=%async_computation.3 | async-start | bytes 2359296 | tf_op jit(solution)/shard_map/all_gather | solution.py:128
  115.6 10.6 %all-to-all-start = ((f32[8,1,1024]{2,1,0:T(1,128)}), f32[8,1,1024]{2,1,0:T(1,128)S(1)}, u32[]{:S(2)}, u32[]{:S(2)}) async-start(f32[8,1,1024]{2,1,0:T(1,128)} %reshape.418), calls=%async_computation | async-start | bytes 65536 | tf_op jit(solution)/shard_map/all_to_all | solution.py:150
  191.5 4.7 %copy-start.2 = (bf16[4,32,1,256]{3,1,2,0:T(8,128)(2,1)S(1)}, bf16[4,32,1,256]{3,1,2,0:T(8,128)(2,1)}, u32[]{:S(2)}) copy-start(bf16[4,32,1,256]{3,1,2,0:T(8,128)(2,1)} %param.10) | copy-start | bytes 196612
  191.5 97.0 %all-to-all-start.2 = ((f32[4,32,8,8,128]{4,3,1,0,2:T(8,128)}), f32[4,32,8,8,128]{4,3,1,0,2:T(8,128)}, u32[]{:S(2)}, u32[]{:S(2)}) async-start(f32[4,32,8,8,128]{4,3,1,0,2:T(8,128)} %bitcast.126), calls=%async_computation.2 | async-start | bytes 8388608 | tf_op jit(solution)/shard_map/all_to_all | solution.py:149
  206.6 6.0 %copy-start.1 = (bf16[4,32,8,128]{3,2,1,0:T(8,128)(2,1)S(1)}, bf16[4,32,8,128]{3,2,1,0:T(8,128)(2,1)}, u32[]{:S(2)}) copy-start(bf16[4,32,8,128]{3,2,1,0:T(8,128)(2,1)} %param.9) | copy-start | bytes 786436
  288.6 3.5 %copy-start = (bf16[64,128,256]{2,1,0:T(8,128)(2,1)S(1)}, bf16[64,128,256]{2,1,0:T(8,128)(2,1)}, u32[]{:S(2)}) copy-start(bf16[64,128,256]{2,1,0:T(8,128)(2,1)} %gather_fusion.5) | copy-start | bytes 12582916
Sparse Core Ops, SparseCore 0:
  9.1 47.2 all-gather.1
where the time goes:
time: 304 us; the launch traced here: 300 us
  waiting for transfers between devices  97.6 us (32%)
  blocking collectives  80.1 us (26%)
  local copies, waits for them, and re-layouts  35 us (12%)
  matrix products  32.5 us (11%)
  other arithmetic  32.3 us (11%)
  between operations  14.3 us (5%)
  starting transfers between devices  8.4 us (3%)
    all_to_all x1, waiting for transfers between devices, per_device(): lax.all_to_all(shares_out, 'pre', split_axis=2, concat_axis=2, tiled=True)  72 us
    all_to_all x1, blocking collectives, per_device(): lax.all_to_all(outgoing, 'rep', split_axis=0, concat_axis=0, tiled=True)  65.4 us
    all_gather x1, waiting for transfers between devices, per_device(): gathered = lax.all_gather(queries, 'pre', axis=2, tiled=True)  22.5 us
    dot_general x8, matrix products, per_head(): jnp.dot(weights.astype(jnp.bfloat16), head_kv[:, head_dim:], preferred_el...  18.4 us
    reduce_sum x8, other arithmetic, per_head(): weight_sum = jnp.sum(weights, axis=1)  15.5 us
    unnamed x1, blocking collectives  14.7 us
    dot_general x8, matrix products, per_head(): lax.dot_general(block_of_queries, head_kv[:, :head_dim], (((1,), (1,)), (...  10.6 us
    squeeze x8, local copies, waits for them, and re-layouts, prefix_partial(): partial_value, log_total = lax.map(per_head, (query_rows, prefix_kv))  10.4 us
  transfers between devices with their start and end apart: 3, of which 3 were waited for; matrix products, arithmetic and copies ran while one was open for 12% of the time, Pallas kernels for 0%

commit v1 on v0

v1 whole, which is shorter than its diff:
```python
import functools

import jax
import jax.numpy as jnp
from jax import lax
from jax.experimental import pallas as pl
from jax.experimental.pallas import tpu as pltpu
from jax.sharding import PartitionSpec as P

MESH = pl.DeviceIdType.MESH
BF16 = jnp.bfloat16
F32 = jnp.float32
I32 = jnp.int32

N_REP, N_PRE = 32, 8
X_SIZE, Y_SIZE = 4, 4
TOKENS = 2048
HALF = TOKENS // 2
QUARTER = HALF // 4
AGENTS = 32
ROWS = 32
HEAD = 128
PAGE = 128
POOL = 56
MSG = 64
BLOCK = 256
BLOCKS = AGENTS * ROWS // BLOCK
CHUNK = 256
TO_LOG2 = HEAD ** (-0.5) * 1.4426950408889634
LOW = -1e30


def kernel(
    local_ref, arr_row_ref, arr_col_ref, arrival_ref, table_ref, pages_ref, prefix_ref, pool_hbm,
    out_ref,
    kv, pool, asked, req_out, meta, idx_v, idx_s, res, res_lse, ans_out, ans_in,
    s0, s1, m0, m1, acc, m_run, l_run,
    zs, zr, xs, xr, ss, sr, rqs, rqr, mts, mtr, rps, rpr, loc,
):
    rep = lax.axis_index("rep")
    pre = lax.axis_index("pre")
    core = lax.rem(rep, 2)
    x = lax.rem(rep // 2, X_SIZE)
    y = rep // (2 * X_SIZE)
    sibling = rep + 1 - 2 * core

    def at_xy(xx, yy):
        return (lax.rem(yy + Y_SIZE, Y_SIZE) * X_SIZE + lax.rem(xx + X_SIZE, X_SIZE)) * 2 + core

    x_up, x_down = at_xy(x + 1, y), at_xy(x - 1, y)
    y_up, y_down = at_xy(x, y + 1), at_xy(x, y - 1)
    mine = lax.rem(x + 2 * y, 4)

    def spot(which, size=QUARTER, extra=0):
        start = core * HALF + lax.rem(which + 4, 4) * QUARTER + extra
        return pl.ds(pl.multiple_of(start, 128), size)

    def shard_of(k):
        far = (k + 1) // 2
        return lax.rem(pre + jnp.where(lax.rem(k, 2) == 1, far, -far) + N_PRE, N_PRE)

    def z_send(plane):
        where = spot(mine)
        return pltpu.make_async_remote_copy(
            src_ref=prefix_ref.at[plane, where, :], dst_ref=kv.at[pre, where, :],
            send_sem=zs.at[plane], recv_sem=zr.at[pre], device_id=(rep, plane), device_id_type=MESH)

    def z_recv(p):
        where = spot(mine)
        return pltpu.make_async_remote_copy(
            src_ref=kv.at[p, where, :], dst_ref=kv.at[p, where, :],
            send_sem=zs.at[p], recv_sem=zr.at[p], device_id=(rep, p), device_id_type=MESH)

    def xy_copies(p, which, who):
        out = []
        for i, (size, extra) in enumerate(
            ((QUARTER, 0), (QUARTER, 0), (QUARTER // 2, 0), (QUARTER // 2, QUARTER // 2))
        ):
            ref = kv.at[p, spot(which[i], size, extra), :]
            out.append(pltpu.make_async_remote_copy(
                src_ref=ref, dst_ref=ref, send_sem=xs.at[p, i], recv_sem=xr.at[p, i],
                device_id=(who[i], pre), device_id_type=MESH))
        return out

    def xy_send(p):
        return xy_copies(p, (mine, mine, mine, mine), (x_up, x_down, y_up, y_down))

    def xy_recv(p):
        return xy_copies(p, (mine - 1, mine + 1, mine + 2, mine + 2), (x_down, x_up, y_down, y_up))

    def sib_copy(p, half):
        ref = kv.at[p, pl.ds(pl.multiple_of(half * HALF, HALF), HALF), :]
        return pltpu.make_async_remote_copy(
            src_ref=ref, dst_ref=ref, send_sem=ss.at[p], recv_sem=sr.at[p],
            device_id=(sibling, pre), device_id_type=MESH)

    def request(src_slot, dst_slot, other):
        return pltpu.make_async_remote_copy(
            src_ref=req_out.at[src_slot], dst_ref=asked.at[dst_slot],
            send_sem=rqs.at[src_slot], recv_sem=rqr.at[dst_slot], device_id=(other, pre), device_id_type=MESH)

    def tell(dst_slot, send_slot, other):
        return pltpu.make_async_remote_copy(
            src_ref=arr_row_ref, dst_ref=meta.at[dst_slot],
            send_sem=mts.at[send_slot], recv_sem=mtr.at[dst_slot], device_id=(other, pre), device_id_type=MESH)

    def answer(src_slot, dst_slot, other):
        return pltpu.make_async_remote_copy(
            src_ref=ans_out.at[src_slot], dst_ref=ans_in.at[dst_slot],
            send_sem=rps.at[src_slot], recv_sem=rpr.at[dst_slot], device_id=(other, pre), device_id_type=MESH)

    def peers(fn):
        def one(i, c):
            fn(lax.rem(rep + i, N_REP))
            return c
        lax.fori_loop(1, N_REP, one, 0)

    def planes(fn):
        def one(k, c):
            fn(shard_of(k))
            return c
        lax.fori_loop(1, N_PRE, one, 0)

    own = pltpu.make_async_copy(prefix_ref.at[pre], kv.at[pre], loc.at[0])
    own.start()
    pool_copy = pltpu.make_async_copy(pool_hbm, pool, loc.at[1])
    pool_copy.start()
    barrier = pltpu.get_barrier_semaphore()
    peers(lambda o: pl.semaphore_signal(barrier, inc=1, device_id=(o, pre), device_id_type=MESH))
    planes(lambda p: pl.semaphore_signal(barrier, inc=1, device_id=(rep, p), device_id_type=MESH))

    lane = lax.broadcasted_iota(I32, (AGENTS, HEAD), 1)
    sub = lax.broadcasted_iota(I32, (AGENTS, HEAD), 0)
    from_rep = lax.shift_right_logical(arr_col_ref[...], 5)
    asker = jnp.max(jnp.where(from_rep == lane, sub, 0), axis=0, keepdims=True)
    idx_v[...] = jnp.broadcast_to(asker, (8, HEAD))
    put = pltpu.make_async_copy(idx_v, idx_s, loc.at[2])
    put.start()
    put.wait()

    pl.semaphore_wait(barrier, N_REP - 1 + N_PRE - 1)
    planes(lambda p: z_send(p).start())

    def ask(o):
        tell(rep, o, o).start()
        req_out[o] = local_ref[idx_s[0, o]]
        request(o, rep, o).start()
    peers(ask)
    asked[rep] = local_ref[0]
    meta[rep] = arr_row_ref[...]
    ans_in[rep] = jnp.zeros((ROWS, 2 * HEAD), BF16)

    m_run[...] = jnp.full_like(m_run, LOW)
    l_run[...] = jnp.zeros_like(l_run)
    acc[...] = jnp.zeros_like(acc)
    score_bufs, peak_bufs = (s0, s1), (m0, m1)
    per = BLOCK // ROWS

    def block_queries(b):
        return local_ref[b * per:(b + 1) * per, :ROWS, :].reshape(BLOCK, HEAD)

    def score_chunk(q, p, u, kc, peak):
        k = kv[p, kc * CHUNK:(kc + 1) * CHUNK, :HEAD]
        s = lax.dot_general(q, k, (((1,), (1,)), ((), ())), preferred_element_type=F32)
        score_bufs[u][:, kc * CHUNK:(kc + 1) * CHUNK] = s
        for j in range(CHUNK // 128):
            part = s[:, j * 128:(j + 1) * 128]
            peak = part if peak is None else jnp.maximum(peak, part)
        return peak

    def keep_peak(u, peak):
        peak_bufs[u][...] = jnp.broadcast_to(jnp.max(peak, axis=1, keepdims=True), (BLOCK, 128))

    def step(b, p, b_next, p_next):
        u, v = b % 2, b_next % 2
        q = block_queries(b_next)
        peak = peak_bufs[u][:, :1]
        nxt = None
        total = None
        out = None
        for kc in range(TOKENS // CHUNK):
            nxt = score_chunk(q, p_next, v, kc, nxt)
            w = jnp.exp2((score_bufs[u][:, kc * CHUNK:(kc + 1) * CHUNK] - peak) * TO_LOG2)
            for j in range(CHUNK // 128):
                part = w[:, j * 128:(j + 1) * 128]
                total = part if total is None else total + part
            d = jnp.dot(w.astype(BF16), kv[p, kc * CHUNK:(kc + 1) * CHUNK, HEAD:], preferred_element_type=F32)
            out = d if out is None else out + d
        keep_peak(v, nxt)
        rows = slice(b * BLOCK, (b + 1) * BLOCK)
        total = jnp.sum(total, axis=1, keepdims=True)
        top = peak_bufs[u][...] * TO_LOG2
        old = m_run[rows, :]
        new = jnp.maximum(old, top)
        f_old, f_new = jnp.exp2(old - new), jnp.exp2(top - new)
        m_run[rows, :] = new
        l_run[rows, :] = l_run[rows, :] * f_old + total * f_new
        acc[rows, :] = acc[rows, :] * f_old + out * f_new

    def place_agents():
        peers(lambda o: tell(o, o, o).wait_recv())
        everyone = meta[:, 0, :]
        spots = sub * AGENTS + lane
        rows = []
        for a in range(AGENTS):
            hit = (everyone == rep * AGENTS + a) & (lane < AGENTS)
            rows.append(jnp.max(jnp.where(hit, spots, 0), axis=0, keepdims=True))
        table = jnp.concatenate(rows, axis=0)
        where = jnp.max(table, axis=1, keepdims=True)
        where = jnp.broadcast_to(where, (AGENTS, HEAD))
        leaver = jnp.max(jnp.where(lax.shift_right_logical(where, 5) == lane, sub, 0), axis=0, keepdims=True)
        here = jnp.max(jnp.where(lane == sub, where, 0), axis=0, keepdims=True)
        both = jnp.where(lax.broadcasted_iota(I32, (8, HEAD), 0) == 0, leaver, here)
        idx_v[...] = both
        put.start()
        put.wait()

    def suffix_one(a):
        at = idx_s[1, a]
        src = lax.shift_right_logical(at, 5)
        slot = lax.rem(at, AGENTS)
        msg = jnp.where(src == rep, local_ref[slot], asked[src])
        q, kn, vn = msg[:ROWS], msg[ROWS:ROWS + 16], msg[ROWS + 16:]
        page0, page1 = table_ref[a, 0], table_ref[a, 1]
        dims = (((1,), (1,)), ((), ()))
        c0 = lax.dot_general(q, pool[page0, :, :HEAD], dims, preferred_element_type=F32)
        c1 = lax.dot_general(q, pool[page1, :, :HEAD], dims, preferred_element_type=F32)
        cn = lax.dot_general(q, kn, dims, preferred_element_type=F32)
        c1 = jnp.where(pages_ref[a] > 1, c1, LOW)
        rows_n = lax.broadcasted_iota(I32, (ROWS, 16), 0)
        cols_n = lax.broadcasted_iota(I32, (ROWS, 16), 1)
        cn = jnp.where(cols_n <= lax.shift_right_logical(rows_n, 3), cn, LOW)
        peak = jnp.maximum(
            jnp.max(jnp.maximum(c0, c1), axis=1, keepdims=True), jnp.max(cn, axis=1, keepdims=True))
        w0 = jnp.exp2((c0 - peak) * TO_LOG2)
        w1 = jnp.exp2((c1 - peak) * TO_LOG2)
        wn = jnp.exp2((cn - peak) * TO_LOG2)
        total = jnp.sum(w0 + w1, axis=1, keepdims=True) + jnp.sum(wn, axis=1, keepdims=True)
        o = jnp.dot(w0.astype(BF16), pool[page0, :, HEAD:], preferred_element_type=F32)
        o = o + jnp.dot(w1.astype(BF16), pool[page1, :, HEAD:], preferred_element_type=F32)
        o = o + jnp.dot(wn.astype(BF16), vn, preferred_element_type=F32)
        res[a] = o / total
        res_lse[a] = jnp.broadcast_to(peak * TO_LOG2 + jnp.log2(total), (ROWS, HEAD))

    def suffix_all():
        def some(i, c):
            for j in range(4):
                suffix_one(i * 4 + j)
            return c
        lax.fori_loop(0, AGENTS // 4, some, 0)

    def send_answers():
        lanes = lax.broadcasted_iota(I32, (ROWS, HEAD), 1)

        def one(o):
            a = idx_s[0, o]
            ans_out[o, :, :HEAD] = res[a].astype(BF16)
            lse = res_lse[a]
            hi = lse.astype(BF16).astype(F32)
            mid = (lse - hi).astype(BF16).astype(F32)
            low = lse - hi - mid
            ans_out[o, :, HEAD:] = jnp.where(lanes < 32, hi, jnp.where(lanes < 64, mid, low)).astype(BF16)
            answer(o, rep, o).start()
        peers(one)

    def forward_z(p):
        z_recv(p).wait_recv()
        for c in xy_send(p):
            c.start()

    def forward_xy(p):
        for c in xy_recv(p):
            c.wait_recv()
        sib_copy(p, core).start()

    own.wait()
    peak = None
    q_first = block_queries(0)
    for kc in range(TOKENS // CHUNK):
        peak = score_chunk(q_first, pre, 0, kc, peak)
    keep_peak(0, peak)

    def shard(k, c):
        p = shard_of(k)
        p_next = shard_of(jnp.minimum(k + 1, N_PRE - 1))

        @pl.when((k >= 1) & (k + 2 < N_PRE))
        def _():
            forward_z(shard_of(k + 2))

        step(0, p, 1, p)

        @pl.when((k >= 2) & (k + 1 < N_PRE))
        def _():
            forward_xy(shard_of(k + 1))

        step(1, p, 2, p)
        step(2, p, 3, p)

        @pl.when(k == 0)
        def _():
            forward_z(shard_of(1))
            forward_z(shard_of(2))
            place_agents()
            forward_xy(shard_of(1))
            pool_copy.wait()
            peers(lambda o: request(o, o, o).wait_recv())
            suffix_all()
            forward_xy(shard_of(2))
            send_answers()

        @pl.when(k + 1 < N_PRE)
        def _():
            sib_copy(p_next, 1 - core).wait_recv()

        step(3, p, 0, p_next)
        return c

    lax.fori_loop(0, N_PRE, shard, 0)

    peers(lambda o: answer(o, o, o).wait_recv())

    def finish(i, c):
        for u in range(4):
            j = i * 4 + u
            old = arrival_ref[j]
            src = lax.shift_right_logical(old, 5)
            slot = lax.rem(old, AGENTS)
            got = ans_in[src].astype(F32)
            stays = src == rep
            part = jnp.where(stays, res[slot], got[:, :HEAD])
            lse_got = got[:, HEAD:HEAD + 1] + got[:, HEAD + 32:HEAD + 33] + got[:, HEAD + 64:HEAD + 65]
            lse = jnp.where(stays, res_lse[slot], lse_got)
            rows = pl.ds(pl.multiple_of(j * ROWS, ROWS), ROWS)
            m = m_run[rows, :]
            top = jnp.maximum(m, lse)
            f, g = jnp.exp2(m - top), jnp.exp2(lse - top)
            out_ref[j] = ((acc[rows, :] * f + part * g) / (l_run[rows, :] * f + g)).astype(BF16)
        return c

    lax.fori_loop(0, AGENTS // 4, finish, 0)

    def sent(o):
        tell(rep, o, o).wait_send()
        request(o, rep, o).wait_send()
        answer(o, rep, o).wait_send()
    peers(sent)

    def left(p):
        z_send(p).wait_send()
        for c in xy_send(p):
            c.wait_send()
        sib_copy(p, core).wait_send()
    planes(left)


def attend(local, arr_row, arr_col, arrival, page_table, suffix_pages, prefix_kv, pool):
    vmem = pl.BlockSpec(memory_space=pltpu.VMEM)
    smem = pl.BlockSpec(memory_space=pltpu.SMEM)
    hbm = pl.BlockSpec(memory_space=pl.ANY)
    dma = pltpu.SemaphoreType.DMA
    rows = AGENTS * ROWS
    return pl.pallas_call(
        kernel,
        out_shape=jax.ShapeDtypeStruct((AGENTS, ROWS, HEAD), BF16),
        in_specs=[vmem, vmem, vmem, smem, smem, smem, hbm, hbm],
        out_specs=vmem,
        scratch_shapes=[
            pltpu.VMEM((N_PRE, TOKENS, 2 * HEAD), BF16),
            pltpu.VMEM((POOL, PAGE, 2 * HEAD), BF16),
            pltpu.VMEM((N_REP, MSG, HEAD), BF16),
            pltpu.VMEM((N_REP, MSG, HEAD), BF16),
            pltpu.VMEM((N_REP, 8, HEAD), I32),
            pltpu.VMEM((8, HEAD), I32),
            pltpu.SMEM((8, HEAD), I32),
            pltpu.VMEM((AGENTS, ROWS, HEAD), F32),
            pltpu.VMEM((AGENTS, ROWS, HEAD), F32),
            pltpu.VMEM((N_REP, ROWS, 2 * HEAD), BF16),
            pltpu.VMEM((N_REP, ROWS, 2 * HEAD), BF16),
            pltpu.VMEM((BLOCK, TOKENS), F32),
            pltpu.VMEM((BLOCK, TOKENS), F32),
            pltpu.VMEM((BLOCK, 128), F32),
            pltpu.VMEM((BLOCK, 128), F32),
            pltpu.VMEM((rows, HEAD), F32),
            pltpu.VMEM((rows, HEAD), F32),
            pltpu.VMEM((rows, HEAD), F32),
            dma((N_PRE,)), dma((N_PRE,)),
            dma((N_PRE, 4)), dma((N_PRE, 4)),
            dma((N_PRE,)), dma((N_PRE,)),
            dma((N_REP,)), dma((N_REP,)),
            dma((N_REP,)), dma((N_REP,)),
            dma((N_REP,)), dma((N_REP,)),
            dma((3,)),
        ],
        compiler_params=pltpu.CompilerParams(
            collective_id=0, has_side_effects=True, vmem_limit_bytes=48 << 20),
    )(local, arr_row, arr_col, arrival, page_table, suffix_pages, prefix_kv, pool)


def per_device(queries, newest_key_value, prefix_kv, suffix_pool, page_table, suffix_pages, arrival):
    steps, agents, group, head = queries.shape
    q = queries.transpose(1, 0, 2, 3).reshape(agents, steps * group, head)
    new = newest_key_value[:, :, 0, :].transpose(1, 0, 2)
    new = jnp.pad(new, ((0, 0), (0, 16 - steps), (0, 0)))
    local = jnp.concatenate([q, new[..., :head], new[..., head:]], axis=1)
    arr_row = jnp.broadcast_to(jnp.pad(arrival, (0, head - agents), constant_values=-1)[None, :], (8, head))
    arr_col = jnp.broadcast_to(arrival[:, None], (agents, head))
    pool = suffix_pool.reshape(suffix_pool.shape[0], suffix_pool.shape[2], suffix_pool.shape[3])
    out = attend(local, arr_row, arr_col, arrival, page_table, suffix_pages, prefix_kv, pool)
    return out.reshape(agents, steps, group, head).transpose(1, 0, 2, 3)


def solution(mesh):
    return jax.shard_map(
        per_device,
        mesh=mesh,
        in_specs=(
            P(None, "rep", "pre", None),
            P(None, "rep", "pre", None),
            P(None, "pre", None),
            P("rep", "pre", None, None),
            P("rep", None),
            P("rep"),
            P("rep"),
        ),
        out_specs=P(None, "rep", "pre", None),
        check_vma=False,
    )
```

time: 304 us -> 81.2 us (0.27); the launches traced: 300 us -> 81 us
  waiting for transfers between devices: 97.6 us -> 0 us
  blocking collectives: 80.1 us -> 0 us
  Pallas kernels: 0 us -> 73.6 us
  matrix products: 32.5 us -> 0 us
  other arithmetic: 32.3 us -> 0.06 us
  local copies, waits for them, and re-layouts: 35 us -> 7.28 us
  between operations: 14.3 us -> 0.05 us
  starting transfers between devices: 8.4 us -> 0 us
    all_to_all x2 -> x0, waiting for transfers between devices: 74.4 us -> none  [the longest x1 72 us: per_device(): lax.all_to_all(shares_out, 'pre', split_axis=2, concat_axis=2, tiled=True)]
    pallas_call x0 -> x1, Pallas kernels: none -> 73.6 us  [attend(): pl.pallas_call(kernel, out_shape=jax.ShapeDtypeStruct((AGENTS, ROWS, HEAD...]
    all_to_all x1 -> x0, blocking collectives: 65.4 us -> none  [per_device(): lax.all_to_all(outgoing, 'rep', split_axis=0, concat_axis=0, tiled=True)]
    dot_general x18 -> x0, matrix products: 32.5 us -> none  [the longest x8 18.4 us: per_head(): jnp.dot(weights.astype(jnp.bfloat16), head_kv[:, head_dim:], preferred_el...]
    all_gather x1 -> x0, waiting for transfers between devices: 22.5 us -> none  [per_device(): gathered = lax.all_gather(queries, 'pre', axis=2, tiled=True)]
    reduce_sum x12 -> x0, other arithmetic: 19.3 us -> none  [the longest x8 15.5 us: per_head(): weight_sum = jnp.sum(weights, axis=1)]
    unnamed x1 -> x0, blocking collectives: 14.7 us -> none
    gather x8 -> x0, local copies, waits for them, and re-layouts: 14.2 us -> none  [the longest x1 6.04 us: per_device(): cache_of_suffix = combined[page_index]]
  transfers between devices with their start and end apart: 3 -> 0, of which waited for: 3 -> 0; matrix products, arithmetic and copies ran while one was open for 12% -> 0% of each run, Pallas kernels for 0% -> 0%
where the time goes in v1:
time: 81.2 us; the launch traced here: 81 us
  Pallas kernels  73.6 us (91%)
  local copies, waits for them, and re-layouts  7.28 us (9%)
    pallas_call x1, Pallas kernels, attend(): pl.pallas_call(kernel, out_shape=jax.ShapeDtypeStruct((AGENTS, ROWS, HEAD...  73.6 us
    unnamed x10, local copies, waits for them, and re-layouts  5.05 us

profile of v1, /device:TPU:1, one launch (start us, length us, event | category | flops | bytes accessed | tf_op | source)
XLA Modules:
  0.0 81.0 jit_solution(2408373872860766431)
XLA Ops:
  0.0 0.0 copy-start
  0.0 0.9 %copy.15 = bf16[4,32,1,256]{3,0,1,2:T(4,128)(2,1)S(1)} copy(bf16[4,32,1,256]{3,1,2,0:T(8,128)(2,1)} %param.8) | data formatting | bytes 131072 | tf_op args[1]
  1.0 0.0 copy-done
  1.1 0.1 pad_maximum_fusion.local_ref
  1.1 0.7 broadcast_in_dim.5.arr_col_ref
  1.9 0.8 copy.10.table_ref
  2.6 0.7 pad.9
  3.3 0.0 copy-start.1
  3.3 2.0 %copy-done.1 = bf16[56,1,128,256]{3,2,1,0:T(8,128)(2,1)S(1)} copy-done((bf16[56,1,128,256]{3,2,1,0:T(8,128)(2,1)S(1)}, bf16[56,1,128,256]{3,2,1,0:T(8,128)(2,1)}, u32[]{:S(2)}) %copy-start.1) | copy-done | bytes 3670040
  5.3 0.0 copy-start.2
  5.3 0.7 copy-done.2
  6.0 0.0 copy-start.3
  6.0 0.7 copy-done.3
  6.6 73.6 %shard_map.73 = bf16[32,32,128]{2,1,0:T(8,128)(2,1)S(1)} custom-call(bf16[32,64,128]{2,1,0:T(8,128)(2,1)S(1)} %pad_maximum_fusion.local_ref, s32[8,128]{1,0:T(8,128)S(1)} %broadcast_in_dim.4.arr_row_ref, s32[32,128]{1,0:T(8,128)S(1)} %broadcast_in_dim.5.arr_col_ref, s32[32]{0:T(128)S(1)} %copy-done.2, s32[32,2]{1,0:T(8,128)S(1)} %copy.10.table_ref, ...), custom_call_target="tpu_custom_call" | custom-call | tf_op jit(solution)/shard_map/pallas_call | solution.py:363
  80.2 0.7 copy_bitcast_fusion
  (3 shorter events, 0.1 us)
Async XLA Ops:
  0.0 1.0 %copy-start = (bf16[4,32,8,128]{3,2,1,0:T(8,128)(2,1)S(1)}, bf16[4,32,8,128]{3,2,1,0:T(8,128)(2,1)}, u32[]{:S(2)}) copy-start(bf16[4,32,8,128]{3,2,1,0:T(8,128)(2,1)} %param.7) | copy-start | bytes 786436
  3.3 2.0 %copy-start.1 = (bf16[56,1,128,256]{3,2,1,0:T(8,128)(2,1)S(1)}, bf16[56,1,128,256]{3,2,1,0:T(8,128)(2,1)}, u32[]{:S(2)}) copy-start(bf16[56,1,128,256]{3,2,1,0:T(8,128)(2,1)} %param.10) | copy-start | bytes 11010052
  5.3 0.7 copy-start.2
  6.0 0.7 copy-start.3

commit v2 on v1

v2 whole, which is shorter than its diff:
```python
import functools

import jax
import jax.numpy as jnp
from jax import lax
from jax.experimental import pallas as pl
from jax.experimental.pallas import tpu as pltpu
from jax.sharding import PartitionSpec as P

MESH = pl.DeviceIdType.MESH
BF16 = jnp.bfloat16
F32 = jnp.float32
I32 = jnp.int32

N_REP, N_PRE = 32, 8
X_SIZE, Y_SIZE = 4, 4
TOKENS = 2048
HALF = TOKENS // 2
QUARTER = HALF // 4
AGENTS = 32
ROWS = 32
HEAD = 128
PAGE = 128
POOL = 56
MSG = 48
BLOCK = 256
BLOCKS = AGENTS * ROWS // BLOCK
CHUNK = 256
TO_LOG2 = HEAD ** (-0.5) * 1.4426950408889634
LOW = -1e30


def kernel(
    q_ref, new_ref, arrival_ref, table_ref, pages_ref, prefix_ref, pool_hbm,
    out_ref,
    kv, pool, local, tail, asked, req_out, ask_v, ask_s, idx_v, idx_s, res, res_lse, ans_out, ans_in,
    s0, s1, m0, m1, acc, m_run, l_run,
    zs, zr, xs, xr, ss, sr, rqs, rqr, rps, rpr, loc,
):
    rep = lax.axis_index("rep")
    pre = lax.axis_index("pre")
    core = lax.rem(rep, 2)
    x = lax.rem(rep // 2, X_SIZE)
    y = rep // (2 * X_SIZE)
    sibling = rep + 1 - 2 * core

    def at_xy(xx, yy):
        return (lax.rem(yy + Y_SIZE, Y_SIZE) * X_SIZE + lax.rem(xx + X_SIZE, X_SIZE)) * 2 + core

    x_up, x_down = at_xy(x + 1, y), at_xy(x - 1, y)
    y_up, y_down = at_xy(x, y + 1), at_xy(x, y - 1)
    mine = lax.rem(x + 2 * y, 4)

    def spot(which, size=QUARTER, extra=0):
        start = core * HALF + lax.rem(which + 4, 4) * QUARTER + extra
        return pl.ds(pl.multiple_of(start, 128), size)

    def shard_of(k):
        far = (k + 1) // 2
        return lax.rem(pre + jnp.where(lax.rem(k, 2) == 1, far, -far) + N_PRE, N_PRE)

    def z_send(plane):
        where = spot(mine)
        return pltpu.make_async_remote_copy(
            src_ref=prefix_ref.at[plane, where, :], dst_ref=kv.at[pre, where, :],
            send_sem=zs.at[plane], recv_sem=zr.at[pre], device_id=(rep, plane), device_id_type=MESH)

    def z_recv(p):
        where = spot(mine)
        return pltpu.make_async_remote_copy(
            src_ref=kv.at[p, where, :], dst_ref=kv.at[p, where, :],
            send_sem=zs.at[p], recv_sem=zr.at[p], device_id=(rep, p), device_id_type=MESH)

    def xy_copies(p, which, who):
        out = []
        for i, (size, extra) in enumerate(
            ((QUARTER, 0), (QUARTER, 0), (QUARTER // 2, 0), (QUARTER // 2, QUARTER // 2))
        ):
            ref = kv.at[p, spot(which[i], size, extra), :]
            out.append(pltpu.make_async_remote_copy(
                src_ref=ref, dst_ref=ref, send_sem=xs.at[p], recv_sem=xr.at[p],
                device_id=(who[i], pre), device_id_type=MESH))
        return out

    def xy_send(p):
        return xy_copies(p, (mine, mine, mine, mine), (x_up, x_down, y_up, y_down))

    def xy_all(p):
        ref = kv.at[p, pl.ds(0, 3 * QUARTER), :]
        return pltpu.make_async_remote_copy(
            src_ref=ref, dst_ref=ref, send_sem=xs.at[p], recv_sem=xr.at[p],
            device_id=(x_up, pre), device_id_type=MESH)

    def sib_copy(p, half):
        ref = kv.at[p, pl.ds(pl.multiple_of(half * HALF, HALF), HALF), :]
        return pltpu.make_async_remote_copy(
            src_ref=ref, dst_ref=ref, send_sem=ss.at[p], recv_sem=sr.at[p],
            device_id=(sibling, pre), device_id_type=MESH)

    def request(slot, other):
        return pltpu.make_async_remote_copy(
            src_ref=req_out.at[slot], dst_ref=asked.at[rep],
            send_sem=rqs.at[0], recv_sem=rqr.at[0], device_id=(other, pre), device_id_type=MESH)

    def answer(slot, other):
        return pltpu.make_async_remote_copy(
            src_ref=ans_out.at[slot], dst_ref=ans_in.at[rep],
            send_sem=rps.at[0], recv_sem=rpr.at[0], device_id=(other, pre), device_id_type=MESH)

    def all_of(buf, send, recv):
        ref = buf.at[pl.ds(0, N_REP - 1)]
        return pltpu.make_async_remote_copy(
            src_ref=ref, dst_ref=ref, send_sem=send.at[0], recv_sem=recv.at[0],
            device_id=(sibling, pre), device_id_type=MESH)

    def peers(fn):
        def one(i, c):
            fn(lax.rem(rep + i, N_REP))
            return c
        lax.fori_loop(1, N_REP, one, 0)

    def planes(fn):
        def one(k, c):
            fn(shard_of(k))
            return c
        lax.fori_loop(1, N_PRE, one, 0)

    own = pltpu.make_async_copy(prefix_ref.at[pre], kv.at[pre], loc.at[0])
    own.start()
    pool_copy = pltpu.make_async_copy(pool_hbm, pool, loc.at[1])
    pool_copy.start()
    barrier = pltpu.get_barrier_semaphore()
    peers(lambda o: pl.semaphore_signal(barrier, inc=1, device_id=(o, pre), device_id_type=MESH))
    planes(lambda p: pl.semaphore_signal(barrier, inc=1, device_id=(rep, p), device_id_type=MESH))

    lane = lax.broadcasted_iota(I32, (AGENTS, HEAD), 1)
    sub = lax.broadcasted_iota(I32, (AGENTS, HEAD), 0)
    old = jnp.zeros((AGENTS, HEAD), I32)
    for j in range(AGENTS):
        old = jnp.where(sub == j, arrival_ref[j], old)
    from_rep = lax.shift_right_logical(old, 5)
    asker = jnp.max(jnp.where(from_rep == lane, sub, 0), axis=0, keepdims=True)
    ask_v[...] = jnp.broadcast_to(asker, (8, HEAD))
    ask_put = pltpu.make_async_copy(ask_v, ask_s, loc.at[2])
    ask_put.start()

    for t in range(4):
        tail[:, t, :] = new_ref[t, :, :HEAD].astype(F32)
        tail[:, 4 + t, :] = new_ref[t, :, HEAD:].astype(F32)
    tail[:, 8, :] = (old & 31).astype(F32)
    tail[:, 9, :] = from_rep.astype(F32)
    for t in range(10, 16):
        tail[:, t, :] = jnp.zeros((AGENTS, HEAD), F32)

    def build(i, c):
        for u in range(8):
            j = i * 8 + u
            rows = jnp.concatenate([q_ref[t, j].astype(F32) for t in range(4)] + [tail[j]], axis=0)
            local[j] = rows.astype(BF16)
        return c
    lax.fori_loop(0, AGENTS // 8, build, 0)

    ask_put.wait()
    pl.semaphore_wait(barrier, N_REP - 1 + N_PRE - 1)

    def z_sends(first, last):
        def one(k, c):
            z_send(shard_of(k)).start()
            return c
        lax.fori_loop(first, last, one, 0)
    z_sends(1, 5)

    def ask(o):
        req_out[o] = local[ask_s[0, o]]
        request(o, o).start()
    peers(ask)
    asked[rep] = jnp.zeros((MSG, HEAD), BF16)
    ans_in[rep] = jnp.zeros((ROWS, 2 * HEAD), BF16)

    m_run[...] = jnp.full_like(m_run, LOW)
    l_run[...] = jnp.zeros_like(l_run)
    acc[...] = jnp.zeros_like(acc)
    score_bufs, peak_bufs = (s0, s1), (m0, m1)
    per = BLOCK // ROWS

    def block_queries(b):
        return local[b * per:(b + 1) * per, :ROWS, :].reshape(BLOCK, HEAD)

    def score_chunk(q, p, u, kc, peak):
        k = kv[p, kc * CHUNK:(kc + 1) * CHUNK, :HEAD]
        s = lax.dot_general(q, k, (((1,), (1,)), ((), ())), preferred_element_type=F32)
        score_bufs[u][:, kc * CHUNK:(kc + 1) * CHUNK] = s
        for j in range(CHUNK // 128):
            part = s[:, j * 128:(j + 1) * 128]
            peak = part if peak is None else jnp.maximum(peak, part)
        return peak

    def keep_peak(u, peak):
        peak_bufs[u][...] = jnp.broadcast_to(jnp.max(peak, axis=1, keepdims=True), (BLOCK, 128))

    def step(b, p, b_next, p_next):
        u, v = b % 2, b_next % 2
        q = block_queries(b_next)
        peak = peak_bufs[u][:, :1]
        nxt = None
        total = None
        out = None
        for kc in range(TOKENS // CHUNK):
            nxt = score_chunk(q, p_next, v, kc, nxt)
            w = jnp.exp2((score_bufs[u][:, kc * CHUNK:(kc + 1) * CHUNK] - peak) * TO_LOG2)
            for j in range(CHUNK // 128):
                part = w[:, j * 128:(j + 1) * 128]
                total = part if total is None else total + part
            d = jnp.dot(w.astype(BF16), kv[p, kc * CHUNK:(kc + 1) * CHUNK, HEAD:], preferred_element_type=F32)
            out = d if out is None else out + d
        keep_peak(v, nxt)
        rows = slice(b * BLOCK, (b + 1) * BLOCK)
        total = jnp.sum(total, axis=1, keepdims=True)
        top = peak_bufs[u][...] * TO_LOG2
        old = m_run[rows, :]
        new = jnp.maximum(old, top)
        f_old, f_new = jnp.exp2(old - new), jnp.exp2(top - new)
        m_run[rows, :] = new
        l_run[rows, :] = l_run[rows, :] * f_old + total * f_new
        acc[rows, :] = acc[rows, :] * f_old + out * f_new

    def place_agents():
        all_of(asked, rqs, rqr).wait_recv()
        told = asked[:, ROWS:, :].astype(F32)
        slots = told[:, 8, :].astype(I32)
        reps = told[:, 9, :].astype(I32)
        for_me = (reps == rep) & (sub != rep)
        moved = jnp.where(for_me & (slots == lane), sub, 0)
        stays = jnp.where((from_rep == rep) & ((old & 31) == lane), sub + AGENTS, 0)
        at = jnp.max(jnp.maximum(moved, stays), axis=0, keepdims=True)
        idx_v[:AGENTS, :] = jnp.where(for_me, slots & 31, 0)
        idx_v[AGENTS:, :] = jnp.broadcast_to(at, (8, HEAD))
        put = pltpu.make_async_copy(idx_v, idx_s, loc.at[2])
        put.start()
        put.wait()

    dims = (((1,), (1,)), ((), ()))
    lanes_n = lax.broadcasted_iota(I32, (ROWS, 8), 1)
    steps_n = lax.shift_right_logical(lax.broadcasted_iota(I32, (ROWS, 8), 0), 3)
    lanes_p = lax.broadcasted_iota(I32, (ROWS, 2 * PAGE), 1)

    def suffix_some(agents):
        scored = []
        for a in agents:
            at = idx_s[AGENTS, a]
            msg = jnp.where(at >= AGENTS, local[at & 31], asked[at & 31])
            new = msg[ROWS:].astype(F32)[:8]
            page0, page1 = table_ref[0, a], table_ref[1, a]
            keys = jnp.concatenate([pool[page0, :, :HEAD], pool[page1, :, :HEAD]], axis=0)
            q = msg[:ROWS]
            c = lax.dot_general(q, keys, dims, preferred_element_type=F32)
            cn = lax.dot_general(q, new.astype(BF16), dims, preferred_element_type=F32)
            scored.append((a, page0, page1, new, c, cn))
        weighed = []
        for a, page0, page1, new, c, cn in scored:
            c = jnp.where(lanes_p < pages_ref[a] * PAGE, c, LOW)
            cn = jnp.where(lanes_n <= steps_n, cn, LOW)
            peak = jnp.maximum(jnp.max(c, axis=1, keepdims=True), jnp.max(cn, axis=1, keepdims=True))
            w = jnp.exp2((c - peak) * TO_LOG2)
            wn = jnp.exp2((cn - peak) * TO_LOG2)
            total = jnp.sum(w, axis=1, keepdims=True) + jnp.sum(wn, axis=1, keepdims=True)
            weighed.append((a, page0, page1, new, peak, w.astype(BF16), wn.astype(BF16), total))
        outs = []
        for a, page0, page1, new, peak, w, wn, total in weighed:
            values = jnp.concatenate([pool[page0, :, HEAD:], pool[page1, :, HEAD:]], axis=0)
            newest = jnp.concatenate([new[4:], new[:4]], axis=0).astype(BF16)
            o = jnp.dot(w, values, preferred_element_type=F32)
            o = o + jnp.dot(wn, newest, preferred_element_type=F32)
            outs.append((a, o / total, jnp.broadcast_to(peak * TO_LOG2 + jnp.log2(total), (ROWS, HEAD))))
        for a, o, lse in outs:
            res[a] = o
            res_lse[a] = lse

    def suffix_range(first, last):
        def some(i, c):
            suffix_some([i * 8 + j for j in range(8)])
            return c
        lax.fori_loop(first // 8, last // 8, some, 0)

    def send_answers():
        lanes = lax.broadcasted_iota(I32, (ROWS, HEAD), 1)

        def one(o):
            a = idx_s[o, 0]
            ans_out[o, :, :HEAD] = res[a].astype(BF16)
            lse = res_lse[a]
            hi = lse.astype(BF16).astype(F32)
            mid = (lse - hi).astype(BF16).astype(F32)
            low = lse - hi - mid
            ans_out[o, :, HEAD:] = jnp.where(lanes < 32, hi, jnp.where(lanes < 64, mid, low)).astype(BF16)
            answer(o, o).start()
        peers(one)

    def forward_z(p):
        z_recv(p).wait_recv()
        for c in xy_send(p):
            c.start()

    def forward_xy(p):
        xy_all(p).wait_recv()
        sib_copy(p, core).start()

    own.wait()
    peak = None
    q_first = block_queries(0)
    for kc in range(TOKENS // CHUNK):
        peak = score_chunk(q_first, pre, 0, kc, peak)
    keep_peak(0, peak)

    def shard(k, c):
        p = shard_of(k)
        p_next = shard_of(jnp.minimum(k + 1, N_PRE - 1))

        @pl.when((k == 1) | ((k >= 3) & (k + 2 < N_PRE)))
        def _():
            forward_z(shard_of(jnp.where(k == 1, 4, k + 2)))

        step(0, p, 1, p)

        @pl.when(k == 0)
        def _():
            forward_z(shard_of(1))
            forward_z(shard_of(2))
            z_sends(5, N_PRE)

        @pl.when((k == 1) | ((k >= 3) & (k + 1 < N_PRE)))
        def _():
            forward_xy(shard_of(jnp.where(k == 1, 3, k + 1)))

        step(1, p, 2, p)
        step(2, p, 3, p)

        @pl.when(k == 0)
        def _():
            pool_copy.wait()
            place_agents()
            forward_xy(shard_of(1))
            suffix_range(0, 16)
            forward_z(shard_of(3))
            suffix_range(16, 32)
            forward_xy(shard_of(2))
            send_answers()

        @pl.when(k + 1 < N_PRE)
        def _():
            sib_copy(p_next, 1 - core).wait_recv()

        step(3, p, 0, p_next)
        return c

    lax.fori_loop(0, N_PRE, shard, 0)

    all_of(ans_in, rps, rpr).wait_recv()

    def finish(i, c):
        for u in range(4):
            j = i * 4 + u
            old = arrival_ref[j]
            src = lax.shift_right_logical(old, 5)
            slot = lax.rem(old, AGENTS)
            got = ans_in[src].astype(F32)
            stays = src == rep
            part = jnp.where(stays, res[slot], got[:, :HEAD])
            lse_got = got[:, HEAD:HEAD + 1] + got[:, HEAD + 32:HEAD + 33] + got[:, HEAD + 64:HEAD + 65]
            lse = jnp.where(stays, res_lse[slot], lse_got)
            rows = pl.ds(pl.multiple_of(j * ROWS, ROWS), ROWS)
            m = m_run[rows, :]
            top = jnp.maximum(m, lse)
            f, g = jnp.exp2(m - top), jnp.exp2(lse - top)
            o = (acc[rows, :] * f + part * g) / (l_run[rows, :] * f + g)
            for t in range(4):
                out_ref[t, j] = o[t * 8:(t + 1) * 8].astype(BF16)
        return c

    lax.fori_loop(0, AGENTS // 4, finish, 0)

    all_of(req_out, rqs, rqr).wait_send()
    all_of(ans_out, rps, rpr).wait_send()

    def left(p):
        z_send(p).wait_send()
        xy_all(p).wait_send()
        sib_copy(p, core).wait_send()
    planes(left)


def per_device(queries, newest_key_value, prefix_kv, suffix_pool, page_table, suffix_pages, arrival):
    vmem = pl.BlockSpec(memory_space=pltpu.VMEM)
    smem = pl.BlockSpec(memory_space=pltpu.SMEM)
    hbm = pl.BlockSpec(memory_space=pl.ANY)
    dma = pltpu.SemaphoreType.DMA
    rows = AGENTS * ROWS
    pool = suffix_pool.reshape(suffix_pool.shape[0], suffix_pool.shape[2], suffix_pool.shape[3])
    return pl.pallas_call(
        kernel,
        out_shape=jax.ShapeDtypeStruct(queries.shape, BF16),
        in_specs=[vmem, vmem, smem, smem, smem, hbm, hbm],
        out_specs=vmem,
        scratch_shapes=[
            pltpu.VMEM((N_PRE, TOKENS, 2 * HEAD), BF16),
            pltpu.VMEM((POOL, PAGE, 2 * HEAD), BF16),
            pltpu.VMEM((AGENTS, MSG, HEAD), BF16),
            pltpu.VMEM((AGENTS, 16, HEAD), F32),
            pltpu.VMEM((N_REP, MSG, HEAD), BF16),
            pltpu.VMEM((N_REP, MSG, HEAD), BF16),
            pltpu.VMEM((8, HEAD), I32),
            pltpu.SMEM((8, HEAD), I32),
            pltpu.VMEM((AGENTS + 8, HEAD), I32),
            pltpu.SMEM((AGENTS + 8, HEAD), I32),
            pltpu.VMEM((AGENTS, ROWS, HEAD), F32),
            pltpu.VMEM((AGENTS, ROWS, HEAD), F32),
            pltpu.VMEM((N_REP, ROWS, 2 * HEAD), BF16),
            pltpu.VMEM((N_REP, ROWS, 2 * HEAD), BF16),
            pltpu.VMEM((BLOCK, TOKENS), F32),
            pltpu.VMEM((BLOCK, TOKENS), F32),
            pltpu.VMEM((BLOCK, 128), F32),
            pltpu.VMEM((BLOCK, 128), F32),
            pltpu.VMEM((rows, HEAD), F32),
            pltpu.VMEM((rows, HEAD), F32),
            pltpu.VMEM((rows, HEAD), F32),
            dma((N_PRE,)), dma((N_PRE,)),
            dma((N_PRE,)), dma((N_PRE,)),
            dma((N_PRE,)), dma((N_PRE,)),
            dma((1,)), dma((1,)),
            dma((1,)), dma((1,)),
            dma((3,)),
        ],
        compiler_params=pltpu.CompilerParams(
            collective_id=0, has_side_effects=True, vmem_limit_bytes=60 << 20),
    )(queries, newest_key_value[:, :, 0, :], arrival, page_table.T, suffix_pages, prefix_kv, pool)


def solution(mesh):
    return jax.shard_map(
        per_device,
        mesh=mesh,
        in_specs=(
            P(None, "rep", "pre", None),
            P(None, "rep", "pre", None),
            P(None, "pre", None),
            P("rep", "pre", None, None),
            P("rep", None),
            P("rep"),
            P("rep"),
        ),
        out_specs=P(None, "rep", "pre", None),
        check_vma=False,
    )
```

time: 81.2 us -> 62.6 us (0.77)
  Pallas kernels: 73.6 us -> 60.8 us
  local copies, waits for them, and re-layouts: 7.28 us -> 1.67 us
    pallas_call x1, Pallas kernels: 73.6 us -> 60.8 us  [per_device(): pl.pallas_call(kernel, out_shape=jax.ShapeDtypeStruct(queries.shape, BF16...]
    unnamed x10 -> x1, local copies, waits for them, and re-layouts: 5.05 us -> 1.67 us
where the time goes in v2:
time: 62.6 us; the launch traced here: 62.4 us
  Pallas kernels  60.8 us (97%)
  local copies, waits for them, and re-layouts  1.67 us (3%)
    pallas_call x1, Pallas kernels, per_device(): pl.pallas_call(kernel, out_shape=jax.ShapeDtypeStruct(queries.shape, BF16...  60.8 us
    unnamed x1, local copies, waits for them, and re-layouts  1.67 us

profile of v2, /device:TPU:1, one launch (start us, length us, event | category | flops | bytes accessed | tf_op | source)
XLA Modules:
  0.0 62.4 jit_solution(467100459035193348)
XLA Ops:
  0.0 60.8 %shard_map.73 = bf16[4,32,8,128]{3,2,1,0:T(8,128)(2,1)} custom-call(bf16[4,32,8,128]{3,2,1,0:T(8,128)(2,1)} %q_ref.1, bf16[4,32,256]{2,1,0:T(8,128)(2,1)} %bitcast.4, s32[32]{0:T(128)} %arrival_ref.1, s32[2,32]{1,0:T(2,128)} %bitcast.5, s32[32]{0:T(128)} %pages_ref.1, bf16[8,2048,256]{2,1,0:T(8,128)(2,1)} %prefix_ref.1, bf16[56,128,256]{2,1,0:T(8,128)(2,1)} %bitcast.3), custom_call_target="tpu_custom_call" | custom-call | tf_op jit(solution)/shard_map/pallas_call | solution.py:399
  60.8 1.7 %copy.9 = bf16[4,32,8,128]{3,2,1,0:T(8,128)(2,1)} copy(bf16[4,32,8,128]{3,2,1,0:T(8,128)(2,1)} %shard_map.73) | data formatting | bytes 524288

commit v3 on v2

--- a/solution.py
+++ b/solution.py
@@ -49,13 +49,17 @@
 
     x_up, x_down = at_xy(x + 1, y), at_xy(x - 1, y)
     y_up, y_down = at_xy(x, y + 1), at_xy(x, y - 1)
-    mine = lax.rem(x + 2 * y, 4)
+    swap = core == 1
+    a_up, a_down = jnp.where(swap, y_up, x_up), jnp.where(swap, y_down, x_down)
+    b_up, b_down = jnp.where(swap, x_up, y_up), jnp.where(swap, x_down, y_down)
+    mine = lax.rem(jnp.where(swap, y + 2 * x, x + 2 * y), 4)
 
     def spot(which, size=QUARTER, extra=0):
         start = core * HALF + lax.rem(which + 4, 4) * QUARTER + extra
         return pl.ds(pl.multiple_of(start, 128), size)
 
     def shard_of(k):
+        k = jnp.int32(k)
         far = (k + 1) // 2
         return lax.rem(pre + jnp.where(lax.rem(k, 2) == 1, far, -far) + N_PRE, N_PRE)
 
@@ -83,13 +87,13 @@
         return out
 
     def xy_send(p):
-        return xy_copies(p, (mine, mine, mine, mine), (x_up, x_down, y_up, y_down))
+        return xy_copies(p, (mine, mine, mine, mine), (a_up, a_down, b_up, b_down))
 
     def xy_all(p):
         ref = kv.at[p, pl.ds(0, 3 * QUARTER), :]
         return pltpu.make_async_remote_copy(
             src_ref=ref, dst_ref=ref, send_sem=xs.at[p], recv_sem=xr.at[p],
-            device_id=(x_up, pre), device_id_type=MESH)
+            device_id=(a_up, pre), device_id_type=MESH)
 
     def sib_copy(p, half):
         ref = kv.at[p, pl.ds(pl.multiple_of(half * HALF, HALF), HALF), :]
@@ -144,6 +148,15 @@
     ask_put = pltpu.make_async_copy(ask_v, ask_s, loc.at[2])
     ask_put.start()
 
+    pl.semaphore_wait(barrier, N_REP - 1 + N_PRE - 1)
+
+    def z_sends(first, last):
+        def one(k, c):
+            z_send(shard_of(k)).start()
+            return c
+        lax.fori_loop(first, last, one, 0)
+    z_sends(1, 5)
+
     for t in range(4):
         tail[:, t, :] = new_ref[t, :, :HEAD].astype(F32)
         tail[:, 4 + t, :] = new_ref[t, :, HEAD:].astype(F32)
@@ -161,14 +174,6 @@
     lax.fori_loop(0, AGENTS // 8, build, 0)
 
     ask_put.wait()
-    pl.semaphore_wait(barrier, N_REP - 1 + N_PRE - 1)
-
-    def z_sends(first, last):
-        def one(k, c):
-            z_send(shard_of(k)).start()
-            return c
-        lax.fori_loop(first, last, one, 0)
-    z_sends(1, 5)
 
     def ask(o):
         req_out[o] = local[ask_s[0, o]]
@@ -198,31 +203,39 @@
     def keep_peak(u, peak):
         peak_bufs[u][...] = jnp.broadcast_to(jnp.max(peak, axis=1, keepdims=True), (BLOCK, 128))
 
-    def step(b, p, b_next, p_next):
+    ones = jnp.ones((CHUNK, HEAD), BF16)
+
+    def step(b, p, b_next, p_next, beside=None):
         u, v = b % 2, b_next % 2
         q = block_queries(b_next)
         peak = peak_bufs[u][:, :1]
         nxt = None
-        total = None
         out = None
+
+        def values(kc, w):
+            both = jnp.concatenate([kv[p, kc * CHUNK:(kc + 1) * CHUNK, HEAD:], ones], axis=1)
+            d = jnp.dot(w, both, preferred_element_type=F32)
+            return d if out is None else out + d
+
+        last = None
         for kc in range(TOKENS // CHUNK):
+            w = jnp.exp2((score_bufs[u][:, kc * CHUNK:(kc + 1) * CHUNK] - peak) * TO_LOG2).astype(BF16)
             nxt = score_chunk(q, p_next, v, kc, nxt)
-            w = jnp.exp2((score_bufs[u][:, kc * CHUNK:(kc + 1) * CHUNK] - peak) * TO_LOG2)
-            for j in range(CHUNK // 128):
-                part = w[:, j * 128:(j + 1) * 128]
-                total = part if total is None else total + part
-            d = jnp.dot(w.astype(BF16), kv[p, kc * CHUNK:(kc + 1) * CHUNK, HEAD:], preferred_element_type=F32)
-            out = d if out is None else out + d
+            if last is not None:
+                out = values(kc - 1, last)
+            last = w
+            if beside is not None:
+                beside(kc)
+        out = values(TOKENS // CHUNK - 1, last)
         keep_peak(v, nxt)
         rows = slice(b * BLOCK, (b + 1) * BLOCK)
-        total = jnp.sum(total, axis=1, keepdims=True)
         top = peak_bufs[u][...] * TO_LOG2
         old = m_run[rows, :]
         new = jnp.maximum(old, top)
         f_old, f_new = jnp.exp2(old - new), jnp.exp2(top - new)
         m_run[rows, :] = new
-        l_run[rows, :] = l_run[rows, :] * f_old + total * f_new
-        acc[rows, :] = acc[rows, :] * f_old + out * f_new
+        l_run[rows, :] = l_run[rows, :] * f_old + out[:, HEAD:] * f_new
+        acc[rows, :] = acc[rows, :] * f_old + out[:, :HEAD] * f_new
 
     def place_agents():
         all_of(asked, rqs, rqr).wait_recv()
@@ -282,19 +295,19 @@
             return c
         lax.fori_loop(first // 8, last // 8, some, 0)
 
-    def send_answers():
-        lanes = lax.broadcasted_iota(I32, (ROWS, HEAD), 1)
-
-        def one(o):
-            a = idx_s[o, 0]
-            ans_out[o, :, :HEAD] = res[a].astype(BF16)
-            lse = res_lse[a]
-            hi = lse.astype(BF16).astype(F32)
-            mid = (lse - hi).astype(BF16).astype(F32)
-            low = lse - hi - mid
-            ans_out[o, :, HEAD:] = jnp.where(lanes < 32, hi, jnp.where(lanes < 64, mid, low)).astype(BF16)
-            answer(o, o).start()
-        peers(one)
+    answer_lanes = lax.broadcasted_iota(I32, (ROWS, HEAD), 1)
+
+    def send_answer(i):
+        o = lax.rem(rep + i, N_REP)
+        a = idx_s[o, 0]
+        ans_out[o, :, :HEAD] = res[a].astype(BF16)
+        lse = res_lse[a]
+        hi = lse.astype(BF16).astype(F32)
+        mid = (lse - hi).astype(BF16).astype(F32)
+        low = lse - hi - mid
+        ans_out[o, :, HEAD:] = jnp.where(
+            answer_lanes < 32, hi, jnp.where(answer_lanes < 64, mid, low)).astype(BF16)
+        answer(o, o).start()
 
     def forward_z(p):
         z_recv(p).wait_recv()
@@ -312,54 +325,59 @@
         peak = score_chunk(q_first, pre, 0, kc, peak)
     keep_peak(0, peak)
 
+    def next_arrived(p):
+        sib_copy(p, 1 - core).wait_recv()
+
+    first, second = shard_of(1), shard_of(2)
+    step(0, pre, 1, pre)
+    forward_z(first)
+    forward_z(second)
+    z_sends(5, N_PRE)
+    step(1, pre, 2, pre)
+    step(2, pre, 3, pre)
+    pool_copy.wait()
+    place_agents()
+    forward_z(shard_of(3))
+    forward_z(shard_of(4))
+    forward_xy(first)
+    suffix_range(0, 16)
+    forward_xy(second)
+    suffix_range(16, 32)
+    def all_answers(i, c):
+        send_answer(i)
+        return c
+    lax.fori_loop(1, N_REP, all_answers, 0)
+    next_arrived(first)
+    step(3, pre, 0, first)
+
+    passed = {
+        (1, 1): (forward_xy, 3), (1, 3): (forward_xy, 4),
+        (2, 1): (forward_z, 5), (2, 2): (forward_z, 6),
+        (3, 2): (forward_xy, 5), (4, 0): (forward_z, 7),
+        (4, 1): (forward_xy, 6), (5, 2): (forward_xy, 7),
+    }
+
     def shard(k, c):
         p = shard_of(k)
         p_next = shard_of(jnp.minimum(k + 1, N_PRE - 1))
-
-        @pl.when((k == 1) | ((k >= 3) & (k + 2 < N_PRE)))
-        def _():
-            forward_z(shard_of(jnp.where(k == 1, 4, k + 2)))
-
-        step(0, p, 1, p)
-
-        @pl.when(k == 0)
-        def _():
-            forward_z(shard_of(1))
-            forward_z(shard_of(2))
-            z_sends(5, N_PRE)
-
-        @pl.when((k == 1) | ((k >= 3) & (k + 1 < N_PRE)))
-        def _():
-            forward_xy(shard_of(jnp.where(k == 1, 3, k + 1)))
-
-        step(1, p, 2, p)
-        step(2, p, 3, p)
-
-        @pl.when(k == 0)
-        def _():
-            pool_copy.wait()
-            place_agents()
-            forward_xy(shard_of(1))
-            suffix_range(0, 16)
-            forward_z(shard_of(3))
-            suffix_range(16, 32)
-            forward_xy(shard_of(2))
-            send_answers()
-
-        @pl.when(k + 1 < N_PRE)
-        def _():
-            sib_copy(p_next, 1 - core).wait_recv()
-
-        step(3, p, 0, p_next)
+        for b in range(BLOCKS):
+            for (at, ahead_of), (pass_on, which) in passed.items():
+                if ahead_of == b:
+                    pl.when(k == at)(functools.partial(pass_on, shard_of(which)))
+            if b == BLOCKS - 1:
+                pl.when(k + 1 < N_PRE)(functools.partial(next_arrived, p_next))
+                step(b, p, 0, p_next)
+            else:
+                step(b, p, b + 1, p)
         return c
 
-    lax.fori_loop(0, N_PRE, shard, 0)
+    lax.fori_loop(1, N_PRE, shard, 0)
 
     all_of(ans_in, rps, rpr).wait_recv()
 
     def finish(i, c):
-        for u in range(4):
-            j = i * 4 + u
+        for u in range(8):
+            j = i * 8 + u
             old = arrival_ref[j]
             src = lax.shift_right_logical(old, 5)
             slot = lax.rem(old, AGENTS)
@@ -377,7 +395,7 @@
                 out_ref[t, j] = o[t * 8:(t + 1) * 8].astype(BF16)
         return c
 
-    lax.fori_loop(0, AGENTS // 4, finish, 0)
+    lax.fori_loop(0, AGENTS // 8, finish, 0)
 
     all_of(req_out, rqs, rqr).wait_send()
     all_of(ans_out, rps, rpr).wait_send()

time: 62.6 us -> 56 us (0.89)
  Pallas kernels: 60.8 us -> 53.6 us
    pallas_call x1, Pallas kernels: 60.8 us -> 53.6 us  [per_device(): pl.pallas_call(kernel, out_shape=jax.ShapeDtypeStruct(queries.shape, BF16...]
where the time goes in v3:
time: 56 us; the launch traced here: 55.2 us
  Pallas kernels  53.6 us (96%)
  local copies, waits for them, and re-layouts  1.67 us (3%)
    pallas_call x1, Pallas kernels, per_device(): pl.pallas_call(kernel, out_shape=jax.ShapeDtypeStruct(queries.shape, BF16...  53.6 us
    unnamed x1, local copies, waits for them, and re-layouts  1.67 us

profile of v3, /device:TPU:1, one launch (start us, length us, event | category | flops | bytes accessed | tf_op | source)
XLA Modules:
  0.0 55.2 jit_solution(9615180944328535574)
XLA Ops:
  0.0 53.6 %shard_map.73 = bf16[4,32,8,128]{3,2,1,0:T(8,128)(2,1)} custom-call(bf16[4,32,8,128]{3,2,1,0:T(8,128)(2,1)} %q_ref.1, bf16[4,32,256]{2,1,0:T(8,128)(2,1)} %bitcast.4, s32[32]{0:T(128)} %arrival_ref.1, s32[2,32]{1,0:T(2,128)} %bitcast.5, s32[32]{0:T(128)} %pages_ref.1, bf16[8,2048,256]{2,1,0:T(8,128)(2,1)} %prefix_ref.1, bf16[56,128,256]{2,1,0:T(8,128)(2,1)} %bitcast.3), custom_call_target="tpu_custom_call" | custom-call | tf_op jit(solution)/shard_map/pallas_call | solution.py:417
  53.6 1.7 %copy.9 = bf16[4,32,8,128]{3,2,1,0:T(8,128)(2,1)} copy(bf16[4,32,8,128]{3,2,1,0:T(8,128)(2,1)} %shard_map.73) | data formatting | bytes 524288

commit v4 on v3

--- a/solution.py
+++ b/solution.py
@@ -23,7 +23,7 @@
 PAGE = 128
 POOL = 56
 MSG = 48
-BLOCK = 256
+BLOCK = 512
 BLOCKS = AGENTS * ROWS // BLOCK
 CHUNK = 256
 TO_LOG2 = HEAD ** (-0.5) * 1.4426950408889634
@@ -329,12 +329,10 @@
         sib_copy(p, 1 - core).wait_recv()
 
     first, second = shard_of(1), shard_of(2)
-    step(0, pre, 1, pre)
     forward_z(first)
     forward_z(second)
     z_sends(5, N_PRE)
-    step(1, pre, 2, pre)
-    step(2, pre, 3, pre)
+    step(0, pre, 1, pre)
     pool_copy.wait()
     place_agents()
     forward_z(shard_of(3))
@@ -348,13 +346,13 @@
         return c
     lax.fori_loop(1, N_REP, all_answers, 0)
     next_arrived(first)
-    step(3, pre, 0, first)
+    step(1, pre, 0, first)
 
     passed = {
-        (1, 1): (forward_xy, 3), (1, 3): (forward_xy, 4),
-        (2, 1): (forward_z, 5), (2, 2): (forward_z, 6),
-        (3, 2): (forward_xy, 5), (4, 0): (forward_z, 7),
-        (4, 1): (forward_xy, 6), (5, 2): (forward_xy, 7),
+        (1, 0): (forward_xy, 3), (1, 1): (forward_xy, 4),
+        (2, 0): (forward_z, 5), (2, 1): (forward_z, 6),
+        (3, 1): (forward_xy, 5), (4, 0): (forward_z, 7),
+        (4, 1): (forward_xy, 6), (5, 1): (forward_xy, 7),
     }
 
     def shard(k, c):

time: 56 us -> 54.7 us (0.977); the launches traced: 55.2 us -> 54.6 us
  Pallas kernels: 53.6 us -> 52.9 us
    pallas_call x1, Pallas kernels: 53.6 us -> 52.9 us  [per_device(): pl.pallas_call(kernel, out_shape=jax.ShapeDtypeStruct(queries.shape, BF16...]
where the time goes in v4:
time: 54.7 us; the launch traced here: 54.6 us
  Pallas kernels  52.9 us (97%)
  local copies, waits for them, and re-layouts  1.67 us (3%)
    pallas_call x1, Pallas kernels, per_device(): pl.pallas_call(kernel, out_shape=jax.ShapeDtypeStruct(queries.shape, BF16...  52.9 us
    unnamed x1, local copies, waits for them, and re-layouts  1.67 us

profile of v4, /device:TPU:1, one launch (start us, length us, event | category | flops | bytes accessed | tf_op | source)
XLA Modules:
  0.0 54.6 jit_solution(16230828114654000474)
XLA Ops:
  0.0 52.9 %shard_map.73 = bf16[4,32,8,128]{3,2,1,0:T(8,128)(2,1)} custom-call(bf16[4,32,8,128]{3,2,1,0:T(8,128)(2,1)} %q_ref.1, bf16[4,32,256]{2,1,0:T(8,128)(2,1)} %bitcast.4, s32[32]{0:T(128)} %arrival_ref.1, s32[2,32]{1,0:T(2,128)} %bitcast.5, s32[32]{0:T(128)} %pages_ref.1, bf16[8,2048,256]{2,1,0:T(8,128)(2,1)} %prefix_ref.1, bf16[56,128,256]{2,1,0:T(8,128)(2,1)} %bitcast.3), custom_call_target="tpu_custom_call" | custom-call | tf_op jit(solution)/shard_map/pallas_call | solution.py:415
  52.9 1.7 %copy.9 = bf16[4,32,8,128]{3,2,1,0:T(8,128)(2,1)} copy(bf16[4,32,8,128]{3,2,1,0:T(8,128)(2,1)} %shard_map.73) | data formatting | bytes 524288

commit v5 on v4

--- a/solution.py
+++ b/solution.py
@@ -206,8 +206,10 @@
     ones = jnp.ones((CHUNK, HEAD), BF16)
 
     def step(b, p, b_next, p_next, beside=None):
-        u, v = b % 2, b_next % 2
-        q = block_queries(b_next)
+        u = b % 2
+        if b_next is not None:
+            v = b_next % 2
+            q = block_queries(b_next)
         peak = peak_bufs[u][:, :1]
         nxt = None
         out = None
@@ -220,14 +222,16 @@
         last = None
         for kc in range(TOKENS // CHUNK):
             w = jnp.exp2((score_bufs[u][:, kc * CHUNK:(kc + 1) * CHUNK] - peak) * TO_LOG2).astype(BF16)
-            nxt = score_chunk(q, p_next, v, kc, nxt)
+            if b_next is not None:
+                nxt = score_chunk(q, p_next, v, kc, nxt)
             if last is not None:
                 out = values(kc - 1, last)
             last = w
             if beside is not None:
                 beside(kc)
         out = values(TOKENS // CHUNK - 1, last)
-        keep_peak(v, nxt)
+        if b_next is not None:
+            keep_peak(v, nxt)
         rows = slice(b * BLOCK, (b + 1) * BLOCK)
         top = peak_bufs[u][...] * TO_LOG2
         old = m_run[rows, :]
@@ -357,43 +361,49 @@
 
     def shard(k, c):
         p = shard_of(k)
-        p_next = shard_of(jnp.minimum(k + 1, N_PRE - 1))
+        p_next = shard_of(k + 1)
         for b in range(BLOCKS):
             for (at, ahead_of), (pass_on, which) in passed.items():
                 if ahead_of == b:
                     pl.when(k == at)(functools.partial(pass_on, shard_of(which)))
             if b == BLOCKS - 1:
-                pl.when(k + 1 < N_PRE)(functools.partial(next_arrived, p_next))
+                next_arrived(p_next)
                 step(b, p, 0, p_next)
             else:
                 step(b, p, b + 1, p)
         return c
 
-    lax.fori_loop(1, N_PRE, shard, 0)
-
+    lax.fori_loop(1, N_PRE - 1, shard, 0)
+
+    def finish(j):
+        old = arrival_ref[j]
+        src = lax.shift_right_logical(old, 5)
+        slot = lax.rem(old, AGENTS)
+        got = ans_in[src].astype(F32)
+        stays = src == rep
+        part = jnp.where(stays, res[slot], got[:, :HEAD])
+        lse_got = got[:, HEAD:HEAD + 1] + got[:, HEAD + 32:HEAD + 33] + got[:, HEAD + 64:HEAD + 65]
+        lse = jnp.where(stays, res_lse[slot], lse_got)
+        rows = slice(j * ROWS, (j + 1) * ROWS)
+        m = m_run[rows, :]
+        top = jnp.maximum(m, lse)
+        f, g = jnp.exp2(m - top), jnp.exp2(lse - top)
+        o = (acc[rows, :] * f + part * g) / (l_run[rows, :] * f + g)
+        for t in range(4):
+            out_ref[t, j] = o[t * 8:(t + 1) * 8].astype(BF16)
+
+    last_shard = shard_of(N_PRE - 1)
+    step(0, last_shard, 1, last_shard)
     all_of(ans_in, rps, rpr).wait_recv()
-
-    def finish(i, c):
-        for u in range(8):
-            j = i * 8 + u
-            old = arrival_ref[j]
-            src = lax.shift_right_logical(old, 5)
-            slot = lax.rem(old, AGENTS)
-            got = ans_in[src].astype(F32)
-            stays = src == rep
-            part = jnp.where(stays, res[slot], got[:, :HEAD])
-            lse_got = got[:, HEAD:HEAD + 1] + got[:, HEAD + 32:HEAD + 33] + got[:, HEAD + 64:HEAD + 65]
-            lse = jnp.where(stays, res_lse[slot], lse_got)
-            rows = pl.ds(pl.multiple_of(j * ROWS, ROWS), ROWS)
-            m = m_run[rows, :]
-            top = jnp.maximum(m, lse)
-            f, g = jnp.exp2(m - top), jnp.exp2(lse - top)
-            o = (acc[rows, :] * f + part * g) / (l_run[rows, :] * f + g)
-            for t in range(4):
-                out_ref[t, j] = o[t * 8:(t + 1) * 8].astype(BF16)
-        return c
-
-    lax.fori_loop(0, AGENTS // 8, finish, 0)
+    each = AGENTS // BLOCKS // (TOKENS // CHUNK)
+
+    def finish_some(kc):
+        for j in range(kc * each, (kc + 1) * each):
+            finish(j)
+
+    step(1, last_shard, None, None, finish_some)
+    for j in range(AGENTS // BLOCKS, AGENTS):
+        finish(j)
 
     all_of(req_out, rqs, rqr).wait_send()
     all_of(ans_out, rps, rpr).wait_send()

time: 54.7 us -> 55.2 us (level)
  no operation moved by 1% of the time
where the time goes in v5:
time: 55.2 us; the launch traced here: 55.1 us
  Pallas kernels  53.4 us (97%)
  local copies, waits for them, and re-layouts  1.67 us (3%)
    pallas_call x1, Pallas kernels, per_device(): pl.pallas_call(kernel, out_shape=jax.ShapeDtypeStruct(queries.shape, BF16...  53.4 us
    unnamed x1, local copies, waits for them, and re-layouts  1.67 us

profile of v5, /device:TPU:1, one launch (start us, length us, event | category | flops | bytes accessed | tf_op | source)
XLA Modules:
  0.0 55.1 jit_solution(11595631184857136321)
XLA Ops:
  0.0 53.4 %shard_map.73 = bf16[4,32,8,128]{3,2,1,0:T(8,128)(2,1)} custom-call(bf16[4,32,8,128]{3,2,1,0:T(8,128)(2,1)} %q_ref.1, bf16[4,32,256]{2,1,0:T(8,128)(2,1)} %bitcast.4, s32[32]{0:T(128)} %arrival_ref.1, s32[2,32]{1,0:T(2,128)} %bitcast.5, s32[32]{0:T(128)} %pages_ref.1, bf16[8,2048,256]{2,1,0:T(8,128)(2,1)} %prefix_ref.1, bf16[56,128,256]{2,1,0:T(8,128)(2,1)} %bitcast.3), custom_call_target="tpu_custom_call" | custom-call | tf_op jit(solution)/shard_map/pallas_call | solution.py:425
  53.4 1.7 %copy.9 = bf16[4,32,8,128]{3,2,1,0:T(8,128)(2,1)} copy(bf16[4,32,8,128]{3,2,1,0:T(8,128)(2,1)} %shard_map.73) | data formatting | bytes 524288
